TPU v7x, 128 devices: a whole 4x4x4 slice. The times are simulated.
128 devices in a mesh: col: 32 (over x, y, core), rank: 4 (over z).
Axes of the slice: x: 4, y: 4, z: 4, core: 2. Of those that a mesh axis runs over, the one named last changes fastest.
Arguments:
- coefficients: bfloat16 [16, 32, 64, 16384], P(None, None, None, ('col', 'rank')), may hold values from -6 to 6
- v_factors: bfloat16 [32, 64, 16384], P(None, None, ('col', 'rank')), may hold values from -0.25 to 0.25
- transfer: bfloat16 [3, 32, 32, 64, 128], P(None, None, 'col'), may hold values from -0.75 to 0.75
- u_factors: bfloat16 [32, 64, 16384], P(None, None, ('col', 'rank')), may hold values from -0.75 to 0.75
- orders: int32 [32], replicated, may hold values from 0 to 16383, as said below
- ranks: int32 [32], replicated, may hold values from 16 to 64
Outputs:
- transformed: bfloat16 [16, 32, 64, 16384], P(None, None, None, ('col', 'rank'))
Inputs may be any that keep to these rules, and one draw needn't show every extreme that they name: `orders`: distinct and increasing.
All inputs are finite; a program needn't handle non-finite values.
Results may differ from a plain program's by a relative error of at most 0.007.
Values may be sent and summed in bfloat16 or wider, within the bound.
A program may use at most 128 MiB of HBM per device.

v0:
```python
import jax
import jax.numpy as jnp
from jax import lax
from jax.sharding import PartitionSpec as P


def swapped(value, axis, distance):
    mask = 2**distance
    pairs = [(source, source ^ mask) for source in range(lax.axis_size(axis))]
    return lax.ppermute(value, axis, pairs)


def shards(coefficients, v_factors, transfer, u_factors, orders, ranks):
    width = coefficients.shape[3]
    rank_width = v_factors.shape[1]
    start = (lax.axis_index("col") * lax.axis_size("rank") + lax.axis_index("rank")) * width
    degree = start + lax.iota(jnp.int32, width)
    input_mask = (degree[None, :] >= orders[:, None]).astype(jnp.bfloat16)
    fields_now = coefficients * input_mask[None, :, None, :]
    keep_mask = (lax.iota(jnp.int32, rank_width)[None, :] < ranks[:, None]).astype(jnp.float32)
    nbits = lax.axis_size("col").bit_length() - 1
    partial_value = jnp.einsum(
        "bofw,okw->bofk", fields_now, v_factors, preferred_element_type=jnp.float32
    )
    summed = lax.psum(partial_value, "rank")
    state = (summed * keep_mask[None, :, None, :]).astype(jnp.bfloat16)
    for layer_index in range(transfer.shape[0]):
        partner_bit = nbits - 1 - layer_index
        partner = swapped(state, "col", partner_bit)
        stacked = jnp.concatenate([state, partner], axis=3)
        mixed = jnp.einsum(
            "bofj,okj->bofk",
            stacked,
            transfer[layer_index, :, 0],
            preferred_element_type=jnp.float32,
        )
        state = (mixed * keep_mask[None, :, None, :]).astype(jnp.bfloat16)
    return jnp.einsum(
        "bofk,okw->bofw", state, u_factors, preferred_element_type=jnp.float32
    ).astype(jnp.bfloat16)


def solution(mesh):
    placed = (
        P(None, None, None, ("col", "rank")),
        P(None, None, ("col", "rank")),
        P(None, None, "col", None, None),
        P(None, None, ("col", "rank")),
        P(),
        P(),
    )
    return jax.shard_map(
        shards,
        mesh=mesh,
        in_specs=placed,
        out_specs=P(None, None, None, ("col", "rank")),
        check_vma=False,
    )
```

profile of v0, /device:TPU:0, one launch (start us, length us, event | category | flops | bytes accessed | tf_op | source)
XLA Modules:
  0.0 923.2 jit_solution(15305726110479034224)
XLA Ops:
  6.5 0.0 copy-start
  6.5 0.0 all-reduce.2.cloned.1.call-start
  6.5 0.8 compare_convert_fusion
  7.3 11.5 %convolution_bitcast_fusion = f32[16,32,64,64]{3,2,0,1:T(8,128)} fusion(bf16[32,64,128]{2,1,0:T(8,128)(2,1)} %param.7, bf16[16,32,64,128]{3,2,1,0:T(8,128)(2,1)} %param.6, bf16[32,128]{1,0:T(8,128)(2,1)S(1)} %compare_convert_fusion), kind=kOutput, calls=%fused_computation.4 | convolution fusion | flops 541065216 | bytes 17309696 | tf_op jit(solution)/shard_map/bofw,okw->bofk/dot_general | solution.py:22
  18.8 0.0 copy-start.3
  18.8 0.0 all-reduce.2.cloned.1.call-update
  18.8 0.6 copy-done.3
  19.5 0.1 fusion.30
  19.5 297.6 %all-reduce.2.cloned.1.call-done = f32[16,32,64,64]{3,2,0,1:T(8,128)} async-done(((f32[16,32,64,64]{3,2,0,1:T(8,128)}), f32[16,32,64,64]{3,2,0,1:T(8,128)}) %all-reduce.2.cloned.1.call-update) | async-done | bytes 8388624 | tf_op jit(solution)/shard_map/psum | solution.py:25
  317.2 7.1 multiply_convert_fusion.3
  324.3 3.1 collective-permute-start
  327.4 180.7 %collective-permute-done = bf16[16,32,64,64]{3,2,0,1:T(8,128)(2,1)S(1)} collective-permute-done((bf16[16,32,64,64]{3,2,0,1:T(8,128)(2,1)S(1)}, bf16[16,32,64,64]{3,2,0,1:T(8,128)(2,1)S(1)}, u32[]{:S(2)}, u32[]{:S(2)}) %collective-permute-start) | collective-permute-done | bytes 4194336 | tf_op jit(solution)/shard_map/ppermute | solution.py:10
  508.0 0.0 copy-start.2
  508.0 3.4 copy-done.2
  511.4 7.8 fusion.14
  519.3 1.5 collective-permute-start.1
  520.8 179.9 %collective-permute-done.1 = bf16[16,32,64,64]{3,2,0,1:T(8,128)(2,1)} collective-permute-done((bf16[16,32,64,64]{3,2,0,1:T(8,128)(2,1)S(1)}, bf16[16,32,64,64]{3,2,0,1:T(8,128)(2,1)}, u32[]{:S(2)}, u32[]{:S(2)}) %collective-permute-start.1) | collective-permute-done | bytes 4194336 | tf_op jit(solution)/shard_map/ppermute | solution.py:10
  700.7 7.8 fusion.17
  708.6 0.0 copy-start.1
  708.6 3.4 copy-done.1
  712.0 3.0 collective-permute-start.2
  715.0 178.9 %collective-permute-done.2 = bf16[16,32,64,64]{3,2,0,1:T(8,128)(2,1)} collective-permute-done((bf16[16,32,64,64]{3,2,0,1:T(8,128)(2,1)S(1)}, bf16[16,32,64,64]{3,2,0,1:T(8,128)(2,1)}, u32[]{:S(2)}, u32[]{:S(2)}) %collective-permute-start.2) | collective-permute-done | bytes 4194336 | tf_op jit(solution)/shard_map/ppermute | solution.py:10
  893.9 0.0 copy-done
  893.9 12.7 %convert_bitcast_fusion = bf16[16,32,64,128]{3,2,0,1:T(8,128)(2,1)} fusion(bf16[16,32,64,64]{3,2,0,1:T(8,128)(2,1)} %collective-permute-done.2, bf16[16,32,64,64]{3,2,0,1:T(8,128)(2,1)} %copy-done.1, f32[32,64]{1,0:T(8,128)S(1)} %fusion.30, bf16[32,64,128]{2,1,0:T(8,128)(2,1)S(1)} %copy-done, bf16[3,32,1,64,128]{4,3,2,1,0:T(8,128)(2,1)} %param.8), kind=kOutput, calls=%fused_computation.17 | convolution fusion | flops 1098907648 | bytes 26222592 | tf_op jit(solution)/shard_map/bofk,okw->bofw/dot_general | solution.py:38
  906.6 9.7 %copy.10 = bf16[16,32,64,128]{3,2,1,0:T(8,128)(2,1)} copy(bf16[16,32,64,128]{3,2,0,1:T(8,128)(2,1)} %convert_bitcast_fusion) | data formatting | bytes 16777216 | tf_op jit(solution)/shard_map/convert_element_type | solution.py:40
  (1 shorter events, 0.0 us)
Async XLA Ops:
  6.5 887.4 %copy-start = (bf16[32,64,128]{2,1,0:T(8,128)(2,1)S(1)}, bf16[32,64,128]{2,1,0:T(8,128)(2,1)}, u32[]{:S(2)}) copy-start(bf16[32,64,128]{2,1,0:T(8,128)(2,1)} %param.9) | copy-start | bytes 1572868
  6.5 310.7 %all-reduce.2.cloned.1.call-start = ((), (), s32[]{:S(2)}) async-start(), calls=%async_computation | async-start | bytes 33554432 | tf_op jit(solution)/shard_map/psum | solution.py:25
  18.8 0.7 copy-start.3
  324.3 183.7 %collective-permute-start = (bf16[16,32,64,64]{3,2,0,1:T(8,128)(2,1)S(1)}, bf16[16,32,64,64]{3,2,0,1:T(8,128)(2,1)S(1)}, u32[]{:S(2)}, u32[]{:S(2)}) collective-permute-start(bf16[16,32,64,64]{3,2,0,1:T(8,128)(2,1)S(1)} %multiply_convert_fusion.3), channel_id=1, source_target_pairs={{0,64},{4,68},{8,72},{12,76},{16,80},{20,84},{24,88},{28,92},{32,9... | collective-permute-start | bytes 12582920 | tf_op jit(solution)/shard_map/ppermute | solution.py:10
  508.0 3.4 copy-start.2
  519.3 181.5 %collective-permute-start.1 = (bf16[16,32,64,64]{3,2,0,1:T(8,128)(2,1)S(1)}, bf16[16,32,64,64]{3,2,0,1:T(8,128)(2,1)}, u32[]{:S(2)}, u32[]{:S(2)}) collective-permute-start(bf16[16,32,64,64]{3,2,0,1:T(8,128)(2,1)S(1)} %fusion.14), channel_id=1, source_target_pairs={{0,32},{4,36},{8,40},{12,44},{16,48},{20,52},{24,56},{28,60},{32,0... | collective-permute-start | bytes 12582920 | tf_op jit(solution)/shard_map/ppermute | solution.py:10
  708.6 3.4 copy-start.1
  712.0 182.0 %collective-permute-start.2 = (bf16[16,32,64,64]{3,2,0,1:T(8,128)(2,1)S(1)}, bf16[16,32,64,64]{3,2,0,1:T(8,128)(2,1)}, u32[]{:S(2)}, u32[]{:S(2)}) collective-permute-start(bf16[16,32,64,64]{3,2,0,1:T(8,128)(2,1)S(1)} %fusion.17), channel_id=1, source_target_pairs={{0,16},{4,20},{8,24},{12,28},{16,0},{20,4},{24,8},{28,12},{32,48},... | collective-permute-start | bytes 12582920 | tf_op jit(solution)/shard_map/ppermute | solution.py:10
Sparse Core Ops, SparseCore 0:
  19.0 298.1 all-reduce.1
where the time goes:
time: 923 us
  waiting for transfers between devices  837 us (91%)
  matrix products  39.8 us (4%)
  local copies, waits for them, and re-layouts  17.2 us (2%)
  between operations  13.4 us (1%)
    ppermute x3, waiting for transfers between devices, swapped(): return lax.ppermute(value, axis, pairs)  540 us
    psum x1, waiting for transfers between devices, shards(): summed = lax.psum(partial_value, 'rank')  298 us
  transfers between devices with their start and end apart: 4, of which 4 were waited for; matrix products, arithmetic and copies ran while one was open for 0% of the time, Pallas kernels for 0%

commit v1 on v0

v1 whole, which is shorter than its diff:
```python
import functools

import jax
import jax.numpy as jnp
from jax import lax
from jax.experimental import pallas as pl
from jax.experimental.pallas import tpu as pltpu
from jax.sharding import PartitionSpec as P

MESH = pl.DeviceIdType.MESH
BF16, F32, I32 = jnp.bfloat16, jnp.float32, jnp.int32
QUAD = 4
LAGS = (0, 2, 4, 6, 8, 9, 11, 13)


def dot(a, b, dims=((1,), (0,))):
    return lax.dot_general(a, b, (dims, ((), ())), preferred_element_type=F32)


def spots(plan, g):
    first = [plan[1, QUAD * g + i] for i in range(QUAD)]
    rank = [plan[2, QUAD * g + i] for i in range(QUAD)]
    return first, rank, first[QUAD - 1] + rank[QUAD - 1]


def placing(plan, g, rows, width):
    first, rank, _ = spots(plan, g)
    lane = lax.broadcasted_iota(I32, (1, QUAD * width), 1)
    target = jnp.full((1, QUAD * width), -1, I32)
    for i in range(QUAD):
        k = lane - i * width
        here = (k >= 0) & (k < rank[i])
        target = jnp.where(here, first[i] + k, target)
    row = lax.broadcasted_iota(I32, (rows, QUAD * width), 0)
    return jnp.where(row == target, 1.0, 0.0).astype(BF16)


def order_of(plan, g, index):
    first, _, _ = spots(plan, g)
    seg = jnp.zeros(index.shape, I32)
    for i in range(1, QUAD):
        seg = seg + jnp.where(index >= first[i], 1, 0)
    return seg


def mixing(rows, levels, lags, plan, x, v, t, out, a, place, maps, far, far_in, near, near_in, summed, summed_in,
           keep_next, keep_own, state, state_in, done, send, recv, out_sem):
    col, z = lax.axis_index("col"), lax.axis_index("rank")
    width = v.shape[1]
    chunks = out.shape[0]

    def flipped(bit):
        return col + bit - 2 * bit * lax.rem(lax.div(col, bit), 2)

    def at(step):
        return lax.rem(z + step, 4)

    n_col = lax.axis_size("col")
    partners = [(flipped(n_col >> (l + 1)), z) for l in range(levels)]

    barrier = pltpu.get_barrier_semaphore()
    for peer in [(col, at(1)), (col, at(3))] + partners:
        pl.semaphore_signal(barrier, inc=1, device_id=peer, device_id_type=MESH)
    pl.semaphore_wait(barrier, 2 + levels)

    def remote(kind, j, src, dst, peer):
        return pltpu.make_async_remote_copy(
            src_ref=src, dst_ref=dst, send_sem=send.at[kind, j], recv_sem=recv.at[kind, j],
            device_id=peer, device_id_type=MESH)

    FAR, NEAR, SUM, AHEAD, BACK, ON, LEVEL = 0, 1, 2, 3, 4, 5, 6

    def sides(j):
        h = lax.rem(j, 2)
        return at(1 + 2 * h), at(3 - 2 * h), at(2)

    def far_copy(j):
        ahead, _, _ = sides(j)
        return remote(FAR, j, far.at[j], far_in.at[j], (col, ahead))

    def near_copy(j):
        _, back, _ = sides(j)
        return remote(NEAR, j, near.at[j], near_in.at[j], (col, back))

    def sum_copy(j):
        ahead, _, _ = sides(j)
        return remote(SUM, j, summed.at[j], summed_in.at[j], (col, ahead))

    def level_copy(l, j):
        return remote(LEVEL + l, j, state.at[l, j], state_in.at[l, j], partners[l])

    def ahead_copy(j, q):
        ahead, _, _ = sides(j)
        return remote(AHEAD, j, done.at[j, q], done.at[j, q], (col, ahead))

    def back_copy(j, q):
        _, back, _ = sides(j)
        return remote(BACK, j, done.at[j, q], done.at[j, q], (col, back))

    def on_copy(j, q):
        ahead, _, _ = sides(j)
        return remote(ON, j, done.at[j, q], done.at[j, q], (col, ahead))

    def out_copy(j):
        return pltpu.make_async_copy(done.at[j], out.at[j], out_sem.at[j])

    def leaf(j):
        g, h = lax.div(j, 2), lax.rem(j, 2)
        ahead, back, across = sides(j)

        @pl.when(h == 0)
        def _():
            p = placing(plan, g, rows, width)
            place[...] = p
            degree = (col * 4 + z) * 128 + lax.broadcasted_iota(I32, (1, 128), 1)
            for i in range(QUAD):
                o = plan[0, QUAD * g + i]
                picked = dot(p[:, i * width:(i + 1) * width], v[o])
                kept = jnp.where(degree >= plan[3, QUAD * g + i], picked, 0.0)
                a[:, i * 128:(i + 1) * 128] = kept.astype(BF16)

        def fields(q):
            parts = []
            for b in range(2):
                batch = 4 * q + 2 * h + b
                parts.append(jnp.concatenate([x[batch, plan[0, QUAD * g + i]] for i in range(QUAD)], axis=1))
            return jnp.concatenate(parts, axis=0)

        sent = dot(a[...], jnp.concatenate([fields(across), fields(back)], axis=0), ((1,), (1,)))
        far[j] = sent[:, :128].astype(BF16)
        near[j] = sent[:, 128:].astype(BF16)
        far_copy(j).start()
        near_copy(j).start()
        kept = dot(a[...], jnp.concatenate([fields(ahead), fields(z)], axis=0), ((1,), (1,)))
        keep_next[j] = kept[:, :128]
        keep_own[j] = kept[:, 128:]

        @pl.when(h == 1)
        def _():
            _, _, filled = spots(plan, g)
            first, _, _ = spots(plan, g)
            lane = lax.broadcasted_iota(I32, (1, rows), 1)
            seg = order_of(plan, g, lane)
            k = lane
            for i in range(1, QUAD):
                k = jnp.where(seg == i, lane - first[i], k)
            k = jnp.where(lane < filled, k, -1000)
            j_row = lax.broadcasted_iota(I32, (2 * width, rows), 0)
            pick_own = jnp.where(j_row == k, 1.0, 0.0).astype(BF16)
            pick_partner = jnp.where(j_row - width == k, 1.0, 0.0).astype(BF16)
            row = lax.broadcasted_iota(I32, (rows, rows), 0)
            same = jnp.where(order_of(plan, g, row) == seg, 1.0, 0.0)
            p = place[...]
            for l in range(levels):
                stack = jnp.concatenate([t[l, plan[0, QUAD * g + i], 0] for i in range(QUAD)], axis=0)
                packed = dot(p, stack).astype(BF16)
                maps[l, g, 0] = (dot(packed, pick_own) * same).astype(BF16)
                maps[l, g, 1] = (dot(packed, pick_partner) * same).astype(BF16)

    def pass_on(j):
        far_copy(j).wait_recv()
        summed[j] = (keep_next[j] + far_in[j].astype(F32)).astype(BF16)
        sum_copy(j).start()

    def first_state(j):
        near_copy(j).wait_recv()
        sum_copy(j).wait_recv()
        total = keep_own[j] + near_in[j].astype(F32) + summed_in[j].astype(F32)
        state[0, j] = total.astype(BF16)
        level_copy(0, j).start()

    def mix(l, j):
        g = lax.div(j, 2)
        level_copy(l, j).wait_recv()
        new = dot(maps[l, g, 0], state[l, j]) + dot(maps[l, g, 1], state_in[l, j])
        return new.astype(BF16)

    def level(l, j):
        state[l + 1, j] = mix(l, j)
        level_copy(l + 1, j).start()

    def last_level(j):
        done[j, z] = mix(levels - 1, j)
        ahead_copy(j, z).start()
        back_copy(j, z).start()

    def hand_on(j):
        _, back, _ = sides(j)
        ahead_copy(j, back).wait_recv()
        on_copy(j, back).start()

    def finish(j):
        ahead, _, across = sides(j)
        back_copy(j, ahead).wait_recv()
        on_copy(j, across).wait_recv()
        out_copy(j).start()

    stages = [leaf, pass_on, first_state]
    stages += [functools.partial(level, l) for l in range(levels - 1)]
    stages += [last_level, hand_on, finish]

    def step(s, carry):
        for lag, stage in zip(lags, stages, strict=True):
            j = s - lag

            @pl.when((j >= 0) & (j < chunks))
            def _(stage=stage, j=j):
                stage(j)

        return carry

    lax.fori_loop(0, chunks + max(lags), step, 0)

    def settle(j, carry):
        _, back, _ = sides(j)
        far_copy(j).wait_send()
        near_copy(j).wait_send()
        sum_copy(j).wait_send()
        for l in range(levels):
            level_copy(l, j).wait_send()
        ahead_copy(j, z).wait_send()
        back_copy(j, z).wait_send()
        on_copy(j, back).wait_send()
        out_copy(j).wait()
        return carry

    lax.fori_loop(0, chunks, settle, 0)


def mixed(rows, cid, plan, x, v, t):
    levels, groups = t.shape[0], x.shape[1] // QUAD
    chunks = 2 * groups
    chunk = (chunks, rows, 128)
    kinds = 6 + levels
    vmem, smem, anywhere = (pl.BlockSpec(memory_space=m) for m in (pltpu.VMEM, pltpu.SMEM, pl.ANY))
    return pl.pallas_call(
        functools.partial(mixing, rows, levels, LAGS),
        out_shape=jax.ShapeDtypeStruct((chunks, 4, rows, 128), BF16),
        in_specs=[smem, vmem, vmem, vmem],
        out_specs=anywhere,
        scratch_shapes=[
            pltpu.VMEM((rows, QUAD * 128), BF16),
            pltpu.VMEM((rows, QUAD * v.shape[1]), BF16),
            pltpu.VMEM((levels, groups, 2, rows, rows), BF16),
            pltpu.VMEM(chunk, BF16), pltpu.VMEM(chunk, BF16),
            pltpu.VMEM(chunk, BF16), pltpu.VMEM(chunk, BF16),
            pltpu.VMEM(chunk, BF16), pltpu.VMEM(chunk, BF16),
            pltpu.VMEM(chunk, F32), pltpu.VMEM(chunk, F32),
            pltpu.VMEM((levels, *chunk), BF16), pltpu.VMEM((levels, *chunk), BF16),
            pltpu.VMEM((chunks, 4, rows, 128), BF16),
            pltpu.SemaphoreType.DMA((kinds, chunks)),
            pltpu.SemaphoreType.DMA((kinds, chunks)),
            pltpu.SemaphoreType.DMA((chunks,)),
        ],
        compiler_params=pltpu.CompilerParams(
            collective_id=cid, has_side_effects=True, vmem_limit_bytes=58 * 2**20),
        cost_estimate=pl.CostEstimate(flops=10**9, bytes_accessed=16 * 2**20, transcendentals=0),
    )(plan, x, v, t)


def writing(rows, plan, s, u, out, buf, sem):
    g, groups = pl.program_id(0), pl.num_programs(0)
    slot = lax.rem(g, 2)
    width = u.shape[1]

    def copies(group, slot):
        return [pltpu.make_async_copy(buf.at[slot, i], out.at[:, plan[0, QUAD * group + i]], sem.at[slot, i])
                for i in range(QUAD)]

    p = placing(plan, g, rows, width)
    packed = [dot(p[:, i * width:(i + 1) * width], u[plan[0, QUAD * g + i]]).astype(BF16) for i in range(QUAD)]
    packed = jnp.concatenate(packed, axis=1)

    @pl.when(g >= 2)
    def _():
        for c in copies(g - 2, slot):
            c.wait()

    for h in range(2):
        for q in range(4):
            points = dot(s[h, q], packed, ((0,), (0,))).astype(BF16)
            for i in range(QUAD):
                for b in range(2):
                    buf[slot, i, 4 * q + 2 * h + b] = points[b * 64:(b + 1) * 64, i * 128:(i + 1) * 128]
    for c in copies(g, slot):
        c.start()

    @pl.when(g == groups - 1)
    def _():
        for c in copies(g - 1, 1 - slot) + copies(g, slot):
            c.wait()


def written(rows, plan, s, u, shape):
    groups = shape[1] // QUAD
    return pl.pallas_call(
        functools.partial(writing, rows),
        out_shape=jax.ShapeDtypeStruct(shape, BF16),
        grid_spec=pltpu.PrefetchScalarGridSpec(
            num_scalar_prefetch=1,
            grid=(groups,),
            in_specs=[pl.BlockSpec((2, 4, rows, 128), lambda g, plan: (g, 0, 0, 0)),
                      pl.BlockSpec(memory_space=pltpu.VMEM)],
            out_specs=pl.BlockSpec(memory_space=pl.ANY),
            scratch_shapes=[pltpu.VMEM((2, QUAD, shape[0], shape[2], shape[3]), BF16),
                            pltpu.SemaphoreType.DMA((2, QUAD))],
        ),
        compiler_params=pltpu.CompilerParams(vmem_limit_bytes=48 * 2**20),
    )(plan, s, u)


def shards(coefficients, v_factors, transfer, u_factors, orders, ranks):
    count = orders.shape[0]
    rows = QUAD * v_factors.shape[1]
    perm = lax.iota(I32, count)
    place = ranks.reshape(-1, QUAD)
    first = (jnp.cumsum(place, axis=1) - place).reshape(count)
    plan = jnp.stack([perm, first, ranks, orders])
    s = mixed(rows, 1, plan, coefficients, v_factors, transfer)
    return written(rows, plan, s, u_factors, coefficients.shape)


def solution(mesh):
    placed = (
        P(None, None, None, ("col", "rank")),
        P(None, None, ("col", "rank")),
        P(None, None, "col", None, None),
        P(None, None, ("col", "rank")),
        P(),
        P(),
    )
    return jax.shard_map(
        shards,
        mesh=mesh,
        in_specs=placed,
        out_specs=P(None, None, None, ("col", "rank")),
        check_vma=False,
    )
```

time: 923 us -> 103 us (0.11)
  waiting for transfers between devices: 837 us -> 0 us
  Pallas kernels: 0 us -> 97.9 us
  matrix products: 39.8 us -> 0 us
  local copies, waits for them, and re-layouts: 17.2 us -> 3.06 us
  between operations: 13.4 us -> 0.04 us
    ppermute x3 -> x0, waiting for transfers between devices: 540 us -> none  [swapped(): return lax.ppermute(value, axis, pairs)]
    psum x1 -> x0, waiting for transfers between devices: 298 us -> none  [shards(): summed = lax.psum(partial_value, 'rank')]
    pallas_call x0 -> x2, Pallas kernels: none -> 97.9 us  [the longest x1 90.2 us: mixed(): pl.pallas_call(functools.partial(mixing, rows, levels, LAGS), out_shape=j...]
    dot_general x4 -> x0, matrix products: 39.8 us -> none  [the longest x2 15.6 us: shards(): jnp.einsum('bofj,okj->bofk', stacked, transfer[layer_index, :, 0], prefer...]
    convert_element_type x1 -> x0, local copies, waits for them, and re-layouts: 9.74 us -> none  [shards(): return jnp.einsum('bofk,okw->bofw', state, u_factors, preferred_element_t...]
  transfers between devices with their start and end apart: 4 -> 0, of which waited for: 4 -> 0; matrix products, arithmetic and copies ran while one was open for 0% -> 0% of each run, Pallas kernels for 0% -> 0%
where the time goes in v1:
time: 103 us
  Pallas kernels  97.9 us (95%)
  local copies, waits for them, and re-layouts  3.06 us (3%)
  other arithmetic  2.08 us (2%)
    pallas_call x1, Pallas kernels, mixed(): pl.pallas_call(functools.partial(mixing, rows, levels, LAGS), out_shape=j...  90.2 us
    pallas_call x1, Pallas kernels, written(): pl.pallas_call(functools.partial(writing, rows), out_shape=jax.ShapeDtype...  7.67 us
    unnamed x6, local copies, waits for them, and re-layouts  2.19 us

profile of v1, /device:TPU:0, one launch (start us, length us, event | category | flops | bytes accessed | tf_op | source)
XLA Modules:
  0.0 103.1 jit_solution(6866095582612138151)
XLA Ops:
  0.0 0.0 copy-start.1
  0.0 0.8 reshape.9
  0.8 0.2 reduce_window_sum.13
  1.0 0.1 reduce_window_sum.14
  1.0 0.7 subtract_bitcast_fusion
  1.7 1.3 %pad_add_fusion.plan = s32[4,32]{1,0:T(4,128)} fusion(s32[1,32]{1,0:T(1,128)} %bitcast.5, s32[1,32]{1,0:T(1,128)} %bitcast.4, s32[1,32]{1,0:T(1,128)S(1)} %subtract_bitcast_fusion, s32[1,32]{1,0:T(1,128)S(1)} %iota.4), kind=kLoop, calls=%fused_computation | loop fusion | flops 384 | bytes 1024 | tf_op jit(solution)/shard_map/stack | solution.py:318
  3.0 0.0 copy-start.2
  3.0 90.2 %shard_map.64.s = bf16[16,4,256,128]{3,2,1,0:T(8,128)(2,1)} custom-call(s32[4,32]{1,0:T(4,128)} %pad_add_fusion.plan, bf16[16,32,64,128]{3,2,1,0:T(8,128)(2,1)} %x.1, bf16[32,64,128]{2,1,0:T(8,128)(2,1)} %v.1, bf16[3,32,1,64,128]{4,3,2,1,0:T(8,128)(2,1)} %t.1), custom_call_target="tpu_custom_call" | custom-call | flops 1000000000 | bytes 16777216 | tf_op jit(solution)/shard_map/pallas_call | solution.py:236
  93.2 0.0 copy-done.1
  93.2 0.0 copy-done.2
  93.2 0.0 copy-start
  93.2 2.2 %copy-done = bf16[16,4,256,128]{3,2,1,0:T(8,128)(2,1)S(1)} copy-done((bf16[16,4,256,128]{3,2,1,0:T(8,128)(2,1)S(1)}, bf16[16,4,256,128]{3,2,1,0:T(8,128)(2,1)}, u32[]{:S(2)}) %copy-start) | copy-done | bytes 4194328
  95.4 7.7 %shard_map.65 = bf16[16,32,64,128]{3,2,1,0:T(8,128)(2,1)} custom-call(s32[4,32]{1,0:T(4,128)S(1)} %copy-done.2, bf16[16,4,256,128]{3,2,1,0:T(8,128)(2,1)S(1)} %copy-done, bf16[32,64,128]{2,1,0:T(8,128)(2,1)S(1)} %copy-done.1), custom_call_target="tpu_custom_call" | custom-call | tf_op jit(solution)/shard_map/pallas_call | solution.py:296
  (1 shorter events, 0.0 us)
Async XLA Ops:
  0.0 93.2 %copy-start.1 = (bf16[32,64,128]{2,1,0:T(8,128)(2,1)S(1)}, bf16[32,64,128]{2,1,0:T(8,128)(2,1)}, u32[]{:S(2)}) copy-start(bf16[32,64,128]{2,1,0:T(8,128)(2,1)} %u.1) | copy-start | bytes 1572868
  3.0 90.3 %copy-start.2 = (s32[4,32]{1,0:T(4,128)S(1)}, s32[4,32]{1,0:T(4,128)}, u32[]{:S(2)}) copy-start(s32[4,32]{1,0:T(4,128)} %pad_add_fusion.plan) | copy-start | bytes 1540
  93.2 2.2 %copy-start = (bf16[16,4,256,128]{3,2,1,0:T(8,128)(2,1)S(1)}, bf16[16,4,256,128]{3,2,1,0:T(8,128)(2,1)}, u32[]{:S(2)}) copy-start(bf16[16,4,256,128]{3,2,1,0:T(8,128)(2,1)} %shard_map.64.s) | copy-start | bytes 12582916

commit v2 on v1

--- a/solution.py
+++ b/solution.py
@@ -11,6 +11,7 @@
 BF16, F32, I32 = jnp.bfloat16, jnp.float32, jnp.int32
 QUAD = 4
 LAGS = (0, 2, 4, 6, 8, 9, 11, 13)
+PARTS = (10, 11, 12, 16)
 
 
 def dot(a, b, dims=((1,), (0,))):
@@ -309,15 +310,61 @@
     )(plan, s, u)
 
 
+def turned(row):
+    n = row.shape[1]
+    i, j = (lax.broadcasted_iota(I32, (n, n), d) for d in (0, 1))
+    return jnp.sum(jnp.where(i == j, jnp.broadcast_to(row, (n, n)), 0.0), axis=1, keepdims=True)
+
+
+def planning(heights, orders, ranks, plan, pick):
+    n = ranks.shape[0]
+    groups = n // QUAD
+    i, j = (lax.broadcasted_iota(I32, (n, n), d).astype(F32) for d in (0, 1))
+    lane = lax.broadcasted_iota(I32, (1, n), 1).astype(F32)
+    rank = ranks[...].reshape(1, n).astype(F32)
+    order = orders[...].reshape(1, n).astype(F32)
+    rank_down, order_down = turned(rank), turned(order)
+    ahead = (rank_down > rank) | ((rank_down == rank) & (i < j))
+    spot = jnp.sum(jnp.where(ahead, 1.0, 0.0), axis=0, keepdims=True)
+    turn = sum(jnp.where(spot >= groups * m, 1.0, 0.0) for m in range(1, QUAD))
+    k = spot - groups * turn
+    back = (turn == 1.0) | (turn == 3.0)
+    slot = QUAD * jnp.where(back, groups - 1.0 - k, k) + turn
+    here = turned(slot) == j
+
+    def dealt(values):
+        return jnp.sum(jnp.where(here, values, 0.0), axis=0, keepdims=True)
+
+    rank_here = dealt(rank_down)
+    group = sum(jnp.where(lane >= QUAD * m, 1.0, 0.0) for m in range(1, groups))
+    earlier = (turned(group) == group) & (i < j)
+    first = jnp.sum(jnp.where(earlier, turned(rank_here), 0.0), axis=0, keepdims=True)
+    for at, row in enumerate((dealt(i), first, rank_here, dealt(order_down))):
+        plan[at:at + 1, :] = row.astype(I32)
+    most = jnp.max(first + rank_here)
+    pick[0] = sum((most > height).astype(I32) for height in heights[:-1])
+
+
+def planned(heights, orders, ranks):
+    vmem, smem = (pl.BlockSpec(memory_space=m) for m in (pltpu.VMEM, pltpu.SMEM))
+    return pl.pallas_call(
+        functools.partial(planning, heights),
+        out_shape=(jax.ShapeDtypeStruct((4, ranks.shape[0]), I32), jax.ShapeDtypeStruct((1,), I32)),
+        in_specs=[vmem, vmem],
+        out_specs=(vmem, smem),
+    )(orders, ranks)
+
+
 def shards(coefficients, v_factors, transfer, u_factors, orders, ranks):
-    count = orders.shape[0]
-    rows = QUAD * v_factors.shape[1]
-    perm = lax.iota(I32, count)
-    place = ranks.reshape(-1, QUAD)
-    first = (jnp.cumsum(place, axis=1) - place).reshape(count)
-    plan = jnp.stack([perm, first, ranks, orders])
-    s = mixed(rows, 1, plan, coefficients, v_factors, transfer)
-    return written(rows, plan, s, u_factors, coefficients.shape)
+    most = QUAD * v_factors.shape[1]
+    heights = tuple(most * part // 16 for part in PARTS)
+    plan, pick = planned(heights, orders, ranks)
+
+    def branch(rows, cid, plan, x, v, t, u):
+        return written(rows, plan, mixed(rows, cid, plan, x, v, t), u, x.shape)
+
+    branches = [functools.partial(branch, rows, 1 + at) for at, rows in enumerate(heights)]
+    return lax.switch(pick[0], branches, plan, coefficients, v_factors, transfer, u_factors)
 
 
 def solution(mesh):

time: 103 us -> 89.7 us (0.87)
  Pallas kernels: 97.9 us -> 86.6 us
  other arithmetic: 2.08 us -> 0 us
  local copies, waits for them, and re-layouts: 3.06 us -> 1.81 us
    pallas_call x1, Pallas kernels: 90.2 us -> 77.2 us  [mixed(): pl.pallas_call(functools.partial(mixing, rows, levels, LAGS), out_shape=j...]
    unnamed x6 -> x0, local copies, waits for them, and re-layouts: 2.19 us -> none
    cond x0 -> x4, local copies, waits for them, and re-layouts: none -> 1.81 us
    pallas_call x0 -> x1, Pallas kernels: none -> 1.58 us  [planned(): pl.pallas_call(functools.partial(planning, heights), out_shape=(jax.Shape...]
    another operation x2 -> x0, other arithmetic: 1.41 us -> none  [the longest x1 1.26 us: shards(): plan = jnp.stack([perm, first, ranks, orders])]
where the time goes in v2:
time: 89.7 us; the launch traced here: 89.2 us
  Pallas kernels  86.6 us (97%)
  local copies, waits for them, and re-layouts  1.81 us (2%)
    pallas_call x1, Pallas kernels, mixed(): pl.pallas_call(functools.partial(mixing, rows, levels, LAGS), out_shape=j...  77.2 us
    pallas_call x1, Pallas kernels, written(): pl.pallas_call(functools.partial(writing, rows), out_shape=jax.ShapeDtype...  7.8 us
    cond x4, local copies, waits for them, and re-layouts  1.81 us

profile of v2, /device:TPU:0, one launch (start us, length us, event | category | flops | bytes accessed | tf_op | source)
XLA Modules:
  0.0 89.2 jit_solution(11561042918255765751)
XLA Ops:
  0.0 1.6 %shard_map.68 = (s32[4,32]{1,0:T(4,128)S(1)}, s32[1]{0:T(128)}) custom-call(s32[32]{0:T(128)} %orders.1, s32[32]{0:T(128)} %ranks.1), custom_call_target="tpu_custom_call" | custom-call | tf_op jit(solution)/shard_map/pallas_call | solution.py:350
  2.2 86.9 %conditional.1 = (bf16[16,32,64,128]{3,2,1,0:T(8,128)(2,1)}) conditional(s32[]{:T(128)} %bitcast, (s32[4,32]{1,0:T(4,128)S(1)}, bf16[16,32,64,128]{3,2,1,0:T(8,128)(2,1)}, bf16[32,64,128]{2,1,0:T(8,128)(2,1)}, bf16[3,32,1,64,128]{4,3,2,1,0:T(8,128)(2,1)}, bf16[32,64,128]{2,1,0:T(8,128)(2,1)}) %tuple.17, ...), branch_computations={%region_0.0_spmd, %region_1.0_spmd, %region_2.0_spmd, %region_3.0_... | conditional | flops 1000000000 | bytes 35651648 | solution.py:367
  2.3 0.0 copy-start.5
  2.3 77.2 %branch_1_fun.2.s = bf16[16,4,176,128]{3,2,1,0:T(8,128)(2,1)} custom-call(s32[4,32]{1,0:T(4,128)S(1)} %get-tuple-element.55.plan, bf16[16,32,64,128]{3,2,1,0:T(8,128)(2,1)} %get-tuple-element.56.x, bf16[32,64,128]{2,1,0:T(8,128)(2,1)} %get-tuple-element.57.v, bf16[3,32,1,64,128]{4,3,2,1,0:T(8,128)(2,1)} %get-tuple-element.58.t), custom_call_target="tpu_custom_call" | custom-call | flops 1000000000 | bytes 16777216 | tf_op jit(solution)/shard_map/cond/branch_1_fun/pallas_call | solution.py:237
  79.5 0.0 copy-done.5
  79.5 0.0 copy-start.2
  79.6 1.8 %copy-done.2 = bf16[16,4,176,128]{3,2,1,0:T(8,128)(2,1)S(1)} copy-done((bf16[16,4,176,128]{3,2,1,0:T(8,128)(2,1)S(1)}, bf16[16,4,176,128]{3,2,1,0:T(8,128)(2,1)}, u32[]{:S(2)}) %copy-start.2) | copy-done | bytes 2883608 | tf_op jit(solution)/shard_map/cond
  81.4 7.8 %branch_1_fun.3 = bf16[16,32,64,128]{3,2,1,0:T(8,128)(2,1)} custom-call(s32[4,32]{1,0:T(4,128)S(1)} %get-tuple-element.55.plan, bf16[16,4,176,128]{3,2,1,0:T(8,128)(2,1)S(1)} %copy-done.2, bf16[32,64,128]{2,1,0:T(8,128)(2,1)S(1)} %copy-done.5), custom_call_target="tpu_custom_call" | custom-call | tf_op jit(solution)/shard_map/cond/branch_1_fun/pallas_call | solution.py:297
Async XLA Ops:
  2.3 77.3 %copy-start.5 = (bf16[32,64,128]{2,1,0:T(8,128)(2,1)S(1)}, bf16[32,64,128]{2,1,0:T(8,128)(2,1)}, u32[]{:S(2)}) copy-start(bf16[32,64,128]{2,1,0:T(8,128)(2,1)} %get-tuple-element.59.u) | copy-start | bytes 1572868 | tf_op jit(solution)/shard_map/cond
  79.5 1.8 %copy-start.2 = (bf16[16,4,176,128]{3,2,1,0:T(8,128)(2,1)S(1)}, bf16[16,4,176,128]{3,2,1,0:T(8,128)(2,1)}, u32[]{:S(2)}) copy-start(bf16[16,4,176,128]{3,2,1,0:T(8,128)(2,1)} %branch_1_fun.2.s) | copy-start | bytes 8650756 | tf_op jit(solution)/shard_map/cond

commit v3 on v2

v3 whole, which is shorter than its diff:
```python
import functools
import math

import jax
import jax.numpy as jnp
from jax import lax
from jax.experimental import pallas as pl
from jax.experimental.pallas import tpu as pltpu
from jax.sharding import PartitionSpec as P

MESH = pl.DeviceIdType.MESH
BF16, F32, I32 = jnp.bfloat16, jnp.float32, jnp.int32
QUAD = 4
LAGS = (0, 4, 7, 8, 10, 13, 16, 20, 23)
PARTS = (10, 11, 12, 16)


def dot(a, b, dims=((1,), (0,))):
    return lax.dot_general(a, b, (dims, ((), ())), preferred_element_type=F32)


def spots(plan, g):
    first = [plan[1, QUAD * g + i] for i in range(QUAD)]
    rank = [plan[2, QUAD * g + i] for i in range(QUAD)]
    return first, rank, first[QUAD - 1] + rank[QUAD - 1]


def placing(plan, g, rows, width):
    first, rank, _ = spots(plan, g)
    lane = lax.broadcasted_iota(I32, (1, QUAD * width), 1)
    target = jnp.full((1, QUAD * width), -1, I32)
    for i in range(QUAD):
        k = lane - i * width
        here = (k >= 0) & (k < rank[i])
        target = jnp.where(here, first[i] + k, target)
    row = lax.broadcasted_iota(I32, (rows, QUAD * width), 0)
    return jnp.where(row == target, 1.0, 0.0).astype(BF16)


def order_of(plan, g, index):
    first, _, _ = spots(plan, g)
    seg = jnp.zeros(index.shape, I32)
    for i in range(1, QUAD):
        seg = seg + jnp.where(index >= first[i], 1, 0)
    return seg


def mixing(rows, lags, plan, x_hbm, v_hbm, t_hbm, u_hbm, out, x_first, x_second, v, t, u, a, u_packed, maps, far, far_in, near, near_in,
           summed, summed_in, keep_next, keep_own, blocks, mid, mid_in, done, t_in, send, recv, t_send, t_recv, load_sem):
    col, z = lax.axis_index("col"), lax.axis_index("rank")
    n_col = lax.axis_size("col")
    stride = n_col // 4
    me = lax.div(col, stride)
    half = stride // 2
    width = v.shape[1]
    chunks = done.shape[0]

    def at(step):
        return lax.rem(z + step, 4)

    def ring(step):
        return lax.rem(me + step, 4)

    def block(place):
        return place * stride + lax.rem(col, stride)

    pair = me + 1 - 2 * lax.rem(me, 2)
    opposite = ring(2)
    pair_opposite = lax.rem(pair + 2, 4)
    last = col + half - 2 * half * lax.rem(lax.div(col, half), 2)

    loads = [pltpu.make_async_copy(src, dst, load_sem.at[i]) for i, (src, dst) in enumerate(
        [(v_hbm, v), (x_hbm.at[:, 0], x_first), (x_hbm.at[:, 1], x_second), (t_hbm, t), (u_hbm, u)])]
    for load in loads:
        load.start()

    peers = [(col, at(1)), (col, at(3)), (block(ring(1)), z), (block(ring(3)), z), (last, z)]
    barrier = pltpu.get_barrier_semaphore()
    for peer in peers:
        pl.semaphore_signal(barrier, inc=1, device_id=peer, device_id_type=MESH)
    pl.semaphore_wait(barrier, len(peers))

    t_copy = pltpu.make_async_remote_copy(
        src_ref=t_hbm.at[0], dst_ref=t_in, send_sem=t_send, recv_sem=t_recv,
        device_id=(block(pair), z), device_id_type=MESH)
    t_copy.start()

    def remote(kind, j, src, dst, peer):
        return pltpu.make_async_remote_copy(
            src_ref=src, dst_ref=dst, send_sem=send.at[kind, j], recv_sem=recv.at[kind, j],
            device_id=peer, device_id_type=MESH)

    def sides(j):
        h = lax.rem(j, 2)
        return at(1 + 2 * h), at(3 - 2 * h), at(2)

    def ring_sides(j):
        h = lax.rem(j, 2)
        return ring(1 + 2 * h), ring(3 - 2 * h)

    def far_copy(j):
        ahead, _, _ = sides(j)
        return remote(0, j, far.at[j], far_in.at[j], (col, ahead))

    def near_copy(j):
        _, back, _ = sides(j)
        return remote(1, j, near.at[j], near_in.at[j], (col, back))

    def sum_copy(j):
        ahead, _, _ = sides(j)
        return remote(2, j, summed.at[j], summed_in.at[j], (col, ahead))

    def ahead_copy(j, q):
        ahead, _, _ = sides(j)
        return remote(3, j, done.at[j, q], done.at[j, q], (col, ahead))

    def back_copy(j, q):
        _, back, _ = sides(j)
        return remote(4, j, done.at[j, q], done.at[j, q], (col, back))

    def on_copy(j, q):
        ahead, _, _ = sides(j)
        return remote(5, j, done.at[j, q], done.at[j, q], (col, ahead))

    def ring_ahead(j, c):
        ahead, _ = ring_sides(j)
        return remote(6, j, blocks.at[j, c], blocks.at[j, c], (block(ahead), z))

    def ring_back(j, c):
        _, back = ring_sides(j)
        return remote(7, j, blocks.at[j, c], blocks.at[j, c], (block(back), z))

    def ring_on(j, c):
        ahead, _ = ring_sides(j)
        return remote(8, j, blocks.at[j, c], blocks.at[j, c], (block(ahead), z))

    def mid_copy(j):
        return remote(9, j, mid.at[j], mid_in.at[j], (last, z))

    def leaf(j):
        g, h = lax.div(j, 2), lax.rem(j, 2)
        ahead, back, across = sides(j)

        def halved(x):
            def fields(q):
                return jnp.concatenate([
                    jnp.concatenate([x[q, b, plan[0, QUAD * g + i]] for i in range(QUAD)], axis=1)
                    for b in range(2)], axis=0)

            sent = dot(a[...], jnp.concatenate([fields(across), fields(back)], axis=0), ((1,), (1,)))
            far[j] = sent[:, :128].astype(BF16)
            near[j] = sent[:, 128:].astype(BF16)
            far_copy(j).start()
            near_copy(j).start()
            kept = dot(a[...], jnp.concatenate([fields(ahead), fields(z)], axis=0), ((1,), (1,)))
            keep_next[j] = kept[:, :128]
            keep_own[j] = kept[:, 128:]

        @pl.when(j == 0)
        def _():
            loads[0].wait()

        @pl.when(h == 0)
        def _():
            first, _, _ = spots(plan, g)
            packed = dot(placing(plan, g, rows, width),
                         jnp.concatenate([v[plan[0, QUAD * g + i]] for i in range(QUAD)], axis=0))
            seg = order_of(plan, g, lax.broadcasted_iota(I32, (rows, 1), 0))
            degree = (col * 4 + z) * 128 + lax.broadcasted_iota(I32, (1, 128), 1)
            for i in range(QUAD):
                kept = (seg == i) & (degree >= plan[3, QUAD * g + i])
                a[:, i * 128:(i + 1) * 128] = jnp.where(kept, packed, 0.0).astype(BF16)

        @pl.when(j == 0)
        def _():
            loads[1].wait()

        @pl.when(j == 1)
        def _():
            loads[2].wait()

        @pl.when(h == 0)
        def _():
            halved(x_first)

        @pl.when(h == 1)
        def _():
            halved(x_second)

    def prepare(j):
        g = lax.div(j, 2)

        @pl.when(j == 1)
        def _():
            loads[3].wait()
            loads[4].wait()
            t_copy.wait_recv()

        first, _, filled = spots(plan, g)
        lane = lax.broadcasted_iota(I32, (1, rows), 1)
        seg = order_of(plan, g, lane)
        k = lane
        for i in range(1, QUAD):
            k = jnp.where(seg == i, lane - first[i], k)
        k = jnp.where(lane < filled, k, -1000)
        j_row = lax.broadcasted_iota(I32, (2 * width, rows), 0)
        pick_own = jnp.where(j_row == k, 1.0, 0.0).astype(BF16)
        pick_partner = jnp.where(j_row - width == k, 1.0, 0.0).astype(BF16)
        row = lax.broadcasted_iota(I32, (rows, 1), 0)
        same = order_of(plan, g, row) == seg
        p = placing(plan, g, rows, width)
        u_packed[g] = dot(p, jnp.concatenate([u[plan[0, QUAD * g + i]] for i in range(QUAD)], axis=0)).astype(BF16)
        reads = [lambda o: t[0, o, 0], lambda o: t_in[o, 0], lambda o: t[1, o, 0], lambda o: t[2, o, 0]]
        for m in range(0, 4, 2):
            stack = jnp.concatenate([
                jnp.concatenate([read(plan[0, QUAD * g + i]) for read in reads[m:m + 2]], axis=1)
                for i in range(QUAD)], axis=0)
            packed = dot(p, stack).astype(BF16)
            for n in range(2):
                part = packed[:, n * 2 * width:(n + 1) * 2 * width]
                maps[m + n, g, 0] = jnp.where(same, dot(part, pick_own), 0.0).astype(BF16)
                maps[m + n, g, 1] = jnp.where(same, dot(part, pick_partner), 0.0).astype(BF16)

    def pass_on(j):
        far_copy(j).wait_recv()
        summed[j] = (keep_next[j] + far_in[j].astype(F32)).astype(BF16)
        sum_copy(j).start()

    def first_state(j):
        near_copy(j).wait_recv()
        sum_copy(j).wait_recv()
        total = keep_own[j] + near_in[j].astype(F32) + summed_in[j].astype(F32)
        blocks[j, me] = total.astype(BF16)
        ring_ahead(j, me).start()
        ring_back(j, me).start()

    def ring_hand_on(j):
        _, back = ring_sides(j)
        ring_ahead(j, back).wait_recv()
        ring_on(j, back).start()

    def mix(m, g, own, partner):
        return (dot(maps[m, g, 0], own) + dot(maps[m, g, 1], partner)).astype(BF16)

    def two_levels(j):
        g = lax.div(j, 2)
        for c in (j - 1, j):
            ahead, _ = ring_sides(c)
            ring_back(c, ahead).wait_recv()
            ring_on(c, opposite).wait_recv()

        def both(c):
            return jnp.concatenate([blocks[j - 1, c], blocks[j, c]], axis=1)

        own = mix(0, g, both(me), both(opposite))
        partner = mix(1, g, both(pair), both(pair_opposite))
        new = mix(2, g, own, partner)
        mid[g, 0] = new[:, :128]
        mid[g, 1] = new[:, 128:]
        mid_copy(g).start()

    def last_level(j):
        g = lax.div(j, 2)
        mid_copy(g).wait_recv()
        new = mix(3, g, jnp.concatenate([mid[g, 0], mid[g, 1]], axis=1),
                  jnp.concatenate([mid_in[g, 0], mid_in[g, 1]], axis=1))
        for n, c in enumerate((j - 1, j)):
            done[c, z] = new[:, n * 128:(n + 1) * 128]
            ahead_copy(c, z).start()
            back_copy(c, z).start()

    def hand_on(j):
        _, back, _ = sides(j)
        ahead_copy(j, back).wait_recv()
        on_copy(j, back).start()

    def finish(j):
        ahead, _, across = sides(j)
        back_copy(j, ahead).wait_recv()
        on_copy(j, across).wait_recv()
        g, h = lax.div(j, 2), lax.rem(j, 2)
        seg = order_of(plan, g, lax.broadcasted_iota(I32, (rows, 1), 0))
        factors = u_packed[g]
        factors = jnp.concatenate([jnp.where(seg == i, factors, jnp.zeros_like(factors)) for i in range(QUAD)], axis=1)
        points = dot(jnp.concatenate([done[j, q] for q in range(4)], axis=1), factors, ((0,), (0,))).astype(BF16)
        for q in range(4):
            for b in range(2):
                row = (2 * q + b) * 64
                for i in range(QUAD):
                    out[g, i, 4 * q + 2 * h + b] = points[row:row + 64, i * 128:(i + 1) * 128]

    paired = (prepare, two_levels, last_level)
    stages = (leaf, pass_on, first_state, prepare, ring_hand_on, two_levels, last_level, hand_on, finish)

    def step(s, carry):
        for at in (7, 6, 5, 4, 2, 1, 0, 3, 8):
            lag, stage = lags[at], stages[at]
            j = s - lag
            due = (j >= 0) & (j < chunks)
            if stage in paired:
                due = due & (lax.rem(j, 2) == 1)

            @pl.when(due)
            def _(stage=stage, j=j):
                stage(j)

        return carry

    lax.fori_loop(0, chunks + max(lags), step, 0)

    def settle(j, carry):
        _, back, _ = sides(j)
        _, ring_from = ring_sides(j)
        sent = [far_copy(j), near_copy(j), sum_copy(j), ahead_copy(j, z), back_copy(j, z), on_copy(j, back),
                ring_ahead(j, me), ring_back(j, me), ring_on(j, ring_from)]
        for copy in sent:
            copy.wait_send()

        @pl.when(lax.rem(j, 2) == 1)
        def _():
            mid_copy(lax.div(j, 2)).wait_send()

        return carry

    t_copy.wait_send()
    lax.fori_loop(0, chunks, settle, 0)


def mixed(rows, cid, plan, x, v, t, u):
    batches, orders, fields, points = x.shape
    groups = orders // QUAD
    chunks = 2 * groups
    chunk = (chunks, rows, 128)
    smem, vmem, hbm = (pl.BlockSpec(memory_space=m) for m in (pltpu.SMEM, pltpu.VMEM, pltpu.HBM))
    x = x.reshape(4, 2, batches // 8, orders, fields, points)
    arrays = [
        *[((4, *x.shape[2:]), BF16)] * 2, (v.shape, BF16), (t.shape, BF16), (u.shape, BF16),
        ((rows, QUAD * 128), BF16), ((groups, rows, 128), BF16), ((4, groups, 2, rows, rows), BF16),
        *[(chunk, BF16)] * 6, *[(chunk, F32)] * 2,
        ((chunks, 4, rows, 128), BF16), *[((groups, 2, rows, 128), BF16)] * 2, ((chunks, 4, rows, 128), BF16),
        (t.shape[1:], BF16)]
    size = sum(math.prod(shape[:-1]) * -(-shape[-1] // 128) * 128 * jnp.dtype(kind).itemsize for shape, kind in arrays)
    return pl.pallas_call(
        functools.partial(mixing, rows, LAGS),
        out_shape=jax.ShapeDtypeStruct((groups, QUAD, batches, fields, points), BF16),
        in_specs=[smem, hbm, hbm, hbm, hbm],
        out_specs=vmem,
        scratch_shapes=[
            *[pltpu.VMEM(shape, kind) for shape, kind in arrays],
            pltpu.SemaphoreType.DMA((10, chunks)),
            pltpu.SemaphoreType.DMA((10, chunks)),
            pltpu.SemaphoreType.DMA,
            pltpu.SemaphoreType.DMA,
            pltpu.SemaphoreType.DMA((5,)),
        ],
        compiler_params=pltpu.CompilerParams(
            collective_id=cid, has_side_effects=True, vmem_limit_bytes=size + 13 * 2**20),
        cost_estimate=pl.CostEstimate(flops=10**9, bytes_accessed=16 * 2**20, transcendentals=0),
    )(plan, x, v, t, u)


def dealing(plan, packed, out, sem):
    groups = packed.shape[0]
    copies = [pltpu.make_async_copy(packed.at[g, i], out.at[:, plan[0, QUAD * g + i]], sem.at[g, i])
              for g in range(groups) for i in range(QUAD)]
    for copy in copies:
        copy.start()
    for copy in copies:
        copy.wait()


def dealt_out(plan, packed, shape):
    smem, vmem, hbm = (pl.BlockSpec(memory_space=m) for m in (pltpu.SMEM, pltpu.VMEM, pltpu.HBM))
    return pl.pallas_call(
        dealing,
        out_shape=jax.ShapeDtypeStruct(shape, BF16),
        in_specs=[smem, vmem],
        out_specs=hbm,
        scratch_shapes=[pltpu.SemaphoreType.DMA(packed.shape[:2])],
        compiler_params=pltpu.CompilerParams(vmem_limit_bytes=16 * 2**20),
    )(plan, packed)


def settled(result):
    anywhere = pl.BlockSpec(memory_space=pl.ANY)
    return pl.pallas_call(
        lambda given, out: None,
        out_shape=jax.ShapeDtypeStruct(result.shape, result.dtype),
        in_specs=[anywhere],
        out_specs=anywhere,
        input_output_aliases={0: 0},
    )(result)


def turned(row):
    n = row.shape[1]
    i, j = (lax.broadcasted_iota(I32, (n, n), d) for d in (0, 1))
    return jnp.sum(jnp.where(i == j, jnp.broadcast_to(row, (n, n)), 0.0), axis=1, keepdims=True)


def planning(heights, orders, ranks, plan, pick):
    n = ranks.shape[0]
    groups = n // QUAD
    i, j = (lax.broadcasted_iota(I32, (n, n), d).astype(F32) for d in (0, 1))
    lane = lax.broadcasted_iota(I32, (1, n), 1).astype(F32)
    rank = ranks[...].reshape(1, n).astype(F32)
    order = orders[...].reshape(1, n).astype(F32)
    rank_down, order_down = turned(rank), turned(order)
    ahead = (rank_down > rank) | ((rank_down == rank) & (i < j))
    spot = jnp.sum(jnp.where(ahead, 1.0, 0.0), axis=0, keepdims=True)
    turn = sum(jnp.where(spot >= groups * m, 1.0, 0.0) for m in range(1, QUAD))
    k = spot - groups * turn
    back = (turn == 1.0) | (turn == 3.0)
    slot = QUAD * jnp.where(back, groups - 1.0 - k, k) + turn
    here = turned(slot) == j

    def dealt(values):
        return jnp.sum(jnp.where(here, values, 0.0), axis=0, keepdims=True)

    rank_here = dealt(rank_down)
    group = sum(jnp.where(lane >= QUAD * m, 1.0, 0.0) for m in range(1, groups))
    earlier = (turned(group) == group) & (i < j)
    first = jnp.sum(jnp.where(earlier, turned(rank_here), 0.0), axis=0, keepdims=True)
    for at, row in enumerate((dealt(i), first, rank_here, dealt(order_down))):
        plan[at:at + 1, :] = row.astype(I32)
    most = jnp.max(first + rank_here)
    pick[0] = sum((most > height).astype(I32) for height in heights[:-1])


def planned(heights, orders, ranks):
    vmem, smem = (pl.BlockSpec(memory_space=m) for m in (pltpu.VMEM, pltpu.SMEM))
    return pl.pallas_call(
        functools.partial(planning, heights),
        out_shape=(jax.ShapeDtypeStruct((4, ranks.shape[0]), I32), jax.ShapeDtypeStruct((1,), I32)),
        in_specs=[vmem, vmem],
        out_specs=(vmem, smem),
    )(orders, ranks)


def shards(coefficients, v_factors, transfer, u_factors, orders, ranks):
    most = QUAD * v_factors.shape[1]
    heights = tuple(most * part // 16 for part in PARTS)
    plan, pick = planned(heights, orders, ranks)

    def branch(rows, cid, plan, x, v, t, u):
        return dealt_out(plan, mixed(rows, cid, plan, x, v, t, u), x.shape)

    branches = [functools.partial(branch, rows, 1 + at) for at, rows in enumerate(heights)]
    return settled(lax.switch(pick[0], branches, plan, coefficients, v_factors, transfer, u_factors))


def solution(mesh):
    placed = (
        P(None, None, None, ("col", "rank")),
        P(None, None, ("col", "rank")),
        P(None, None, "col", None, None),
        P(None, None, ("col", "rank")),
        P(),
        P(),
    )
    return jax.shard_map(
        shards,
        mesh=mesh,
        in_specs=placed,
        out_specs=P(None, None, None, ("col", "rank")),
        check_vma=False,
    )
```

time: 89.7 us -> 70 us (0.78)
  Pallas kernels: 86.6 us -> 68.7 us
  local copies, waits for them, and re-layouts: 1.81 us -> 0 us
    pallas_call x2 -> x3, Pallas kernels: 85 us -> 67.1 us  [the longest x1 63 us: mixed(): pl.pallas_call(functools.partial(mixing, rows, LAGS), out_shape=jax.Shape...]
    cond x4 -> x0, local copies, waits for them, and re-layouts: 1.81 us -> none
where the time goes in v3:
time: 70 us; the launch traced here: 69.8 us
  Pallas kernels  68.7 us (98%)
  between operations  0.85 us (1%)
    pallas_call x1, Pallas kernels, mixed(): pl.pallas_call(functools.partial(mixing, rows, LAGS), out_shape=jax.Shape...  63 us
    pallas_call x1, Pallas kernels, dealt_out(): pl.pallas_call(dealing, out_shape=jax.ShapeDtypeStruct(shape, BF16), in_s...  4.11 us
    pallas_call x1, Pallas kernels, planned(): pl.pallas_call(functools.partial(planning, heights), out_shape=(jax.Shape...  1.58 us

profile of v3, /device:TPU:0, one launch (start us, length us, event | category | flops | bytes accessed | tf_op | source)
XLA Modules:
  0.0 69.8 jit_solution(1362581753680453266)
XLA Ops:
  0.0 1.6 %shard_map.64 = (s32[4,32]{1,0:T(4,128)S(1)}, s32[1]{0:T(128)}) custom-call(s32[32]{0:T(128)} %orders.1, s32[32]{0:T(128)} %ranks.1), custom_call_target="tpu_custom_call" | custom-call | tf_op jit(solution)/shard_map/pallas_call | solution.py:432
  2.2 67.4 %conditional.1 = (bf16[16,32,64,128]{3,2,1,0:T(8,128)(2,1)}) conditional(s32[]{:T(128)} %bitcast.4, (bf16[16,32,64,128]{3,2,1,0:T(8,128)(2,1)}, s32[4,32]{1,0:T(4,128)S(1)}, bf16[32,64,128]{2,1,0:T(8,128)(2,1)}, bf16[3,32,1,64,128]{4,3,2,1,0:T(8,128)(2,1)}, bf16[32,64,128]{2,1,0:T(8,128)(2,1)}) %tuple.17, ...), branch_computations={%region_0.0_spmd, %region_1.0_spmd, %region_2.0_spmd, %region_3.0_... | conditional | flops 1000000000 | bytes 50331684 | solution.py:449
  2.3 63.0 %branch_0_fun.2.packed = bf16[8,4,16,64,128]{4,3,2,1,0:T(8,128)(2,1)S(1)} custom-call(s32[4,32]{1,0:T(4,128)S(1)} %get-tuple-element.48.plan, bf16[4,2,2,32,64,128]{5,4,3,2,1,0:T(8,128)(2,1)} %bitcast.5, bf16[32,64,128]{2,1,0:T(8,128)(2,1)} %get-tuple-element.52.v_hbm, bf16[3,32,1,64,128]{4,3,2,1,0:T(8,128)(2,1)} %get-tuple-element.53.t_hbm, ...), custom_call_target="tpu_custom_call" | custom-call | flops 1000000000 | bytes 16777216 | tf_op jit(solution)/shard_map/cond/branch_0_fun/pallas_call | solution.py:343
  65.3 4.1 %branch_0_fun.3 = bf16[16,32,64,128]{3,2,1,0:T(8,128)(2,1)} custom-call(s32[4,32]{1,0:T(4,128)S(1)} %get-tuple-element.48.plan, bf16[8,4,16,64,128]{4,3,2,1,0:T(8,128)(2,1)S(1)} %branch_0_fun.2.packed), custom_call_target="tpu_custom_call" | custom-call | tf_op jit(solution)/shard_map/cond/branch_0_fun/pallas_call | solution.py:374
  (1 shorter events, 0.0 us)

commit v4 on v3

--- a/solution.py
+++ b/solution.py
@@ -11,7 +11,8 @@
 MESH = pl.DeviceIdType.MESH
 BF16, F32, I32 = jnp.bfloat16, jnp.float32, jnp.int32
 QUAD = 4
-LAGS = (0, 4, 7, 8, 10, 13, 16, 20, 23)
+LAGS = (0, 4, 8, 13, 11, 14, 18, 22, 26, 27)
+ORDER = (0, 7, 6, 5, 4, 2, 1, 3, 8, 9)
 PARTS = (10, 11, 12, 16)
 
 
@@ -45,8 +46,9 @@
     return seg
 
 
-def mixing(rows, lags, plan, x_hbm, v_hbm, t_hbm, u_hbm, out, x_first, x_second, v, t, u, a, u_packed, maps, far, far_in, near, near_in,
-           summed, summed_in, keep_next, keep_own, blocks, mid, mid_in, done, t_in, send, recv, t_send, t_recv, load_sem):
+def mixing(rows, lags, plan, x_hbm, v_hbm, t_hbm, u_hbm, out, *scratch):
+    *x, v, t, u, a, u_packed, maps, far, far_in, near, near_in, summed, summed_in, keep_next, keep_own, blocks, mid, mid_in, \
+        done, t_in, send, recv, t_send, t_recv, load_sem = scratch
     col, z = lax.axis_index("col"), lax.axis_index("rank")
     n_col = lax.axis_size("col")
     stride = n_col // 4
@@ -69,8 +71,10 @@
     pair_opposite = lax.rem(pair + 2, 4)
     last = col + half - 2 * half * lax.rem(lax.div(col, half), 2)
 
-    loads = [pltpu.make_async_copy(src, dst, load_sem.at[i]) for i, (src, dst) in enumerate(
-        [(v_hbm, v), (x_hbm.at[:, 0], x_first), (x_hbm.at[:, 1], x_second), (t_hbm, t), (u_hbm, u)])]
+    quarters = [(at(2), at(3 - 2 * h), at(1 + 2 * h), z) for h in range(2)]
+    x_loads = [(x_hbm.at[q, h], x[4 * h + i]) for h in range(2) for i, q in enumerate(quarters[h])]
+    loads = [pltpu.make_async_copy(src, dst, load_sem.at[i])
+             for i, (src, dst) in enumerate([(v_hbm, v), *x_loads, (t_hbm, t), (u_hbm, u)])]
     for load in loads:
         load.start()
 
@@ -139,20 +143,29 @@
 
     def leaf(j):
         g, h = lax.div(j, 2), lax.rem(j, 2)
-        ahead, back, across = sides(j)
-
-        def halved(x):
-            def fields(q):
+
+        def halved(half):
+            parts = x[4 * half:4 * half + 4]
+
+            def fields(part):
                 return jnp.concatenate([
-                    jnp.concatenate([x[q, b, plan[0, QUAD * g + i]] for i in range(QUAD)], axis=1)
+                    jnp.concatenate([part[b, plan[0, QUAD * g + i]] for i in range(QUAD)], axis=1)
                     for b in range(2)], axis=0)
 
-            sent = dot(a[...], jnp.concatenate([fields(across), fields(back)], axis=0), ((1,), (1,)))
+            def leaves(at):
+                @pl.when(j == half)
+                def _():
+                    loads[1 + 4 * half + at].wait()
+                    loads[2 + 4 * half + at].wait()
+
+                return dot(a[...], jnp.concatenate([fields(parts[at]), fields(parts[at + 1])], axis=0), ((1,), (1,)))
+
+            sent = leaves(0)
             far[j] = sent[:, :128].astype(BF16)
             near[j] = sent[:, 128:].astype(BF16)
             far_copy(j).start()
             near_copy(j).start()
-            kept = dot(a[...], jnp.concatenate([fields(ahead), fields(z)], axis=0), ((1,), (1,)))
+            kept = leaves(2)
             keep_next[j] = kept[:, :128]
             keep_own[j] = kept[:, 128:]
 
@@ -171,29 +184,21 @@
                 kept = (seg == i) & (degree >= plan[3, QUAD * g + i])
                 a[:, i * 128:(i + 1) * 128] = jnp.where(kept, packed, 0.0).astype(BF16)
 
-        @pl.when(j == 0)
-        def _():
-            loads[1].wait()
-
-        @pl.when(j == 1)
-        def _():
-            loads[2].wait()
-
         @pl.when(h == 0)
         def _():
-            halved(x_first)
+            halved(0)
 
         @pl.when(h == 1)
         def _():
-            halved(x_second)
+            halved(1)
 
     def prepare(j):
         g = lax.div(j, 2)
 
         @pl.when(j == 1)
         def _():
-            loads[3].wait()
-            loads[4].wait()
+            loads[9].wait()
+            loads[10].wait()
             t_copy.wait_recv()
 
         first, _, filled = spots(plan, g)
@@ -211,15 +216,18 @@
         p = placing(plan, g, rows, width)
         u_packed[g] = dot(p, jnp.concatenate([u[plan[0, QUAD * g + i]] for i in range(QUAD)], axis=0)).astype(BF16)
         reads = [lambda o: t[0, o, 0], lambda o: t_in[o, 0], lambda o: t[1, o, 0], lambda o: t[2, o, 0]]
+        parts = []
         for m in range(0, 4, 2):
             stack = jnp.concatenate([
                 jnp.concatenate([read(plan[0, QUAD * g + i]) for read in reads[m:m + 2]], axis=1)
                 for i in range(QUAD)], axis=0)
             packed = dot(p, stack).astype(BF16)
-            for n in range(2):
-                part = packed[:, n * 2 * width:(n + 1) * 2 * width]
-                maps[m + n, g, 0] = jnp.where(same, dot(part, pick_own), 0.0).astype(BF16)
-                maps[m + n, g, 1] = jnp.where(same, dot(part, pick_partner), 0.0).astype(BF16)
+            parts += [packed[:, :2 * width], packed[:, 2 * width:]]
+        parts = jnp.concatenate(parts, axis=0)
+        for side, pick in enumerate((pick_own, pick_partner)):
+            placed = dot(parts, pick)
+            for m in range(4):
+                maps[m, g, side] = jnp.where(same, placed[m * rows:(m + 1) * rows], 0.0).astype(BF16)
 
     def pass_on(j):
         far_copy(j).wait_recv()
@@ -289,26 +297,7 @@
                 for i in range(QUAD):
                     out[g, i, 4 * q + 2 * h + b] = points[row:row + 64, i * 128:(i + 1) * 128]
 
-    paired = (prepare, two_levels, last_level)
-    stages = (leaf, pass_on, first_state, prepare, ring_hand_on, two_levels, last_level, hand_on, finish)
-
-    def step(s, carry):
-        for at in (7, 6, 5, 4, 2, 1, 0, 3, 8):
-            lag, stage = lags[at], stages[at]
-            j = s - lag
-            due = (j >= 0) & (j < chunks)
-            if stage in paired:
-                due = due & (lax.rem(j, 2) == 1)
-
-            @pl.when(due)
-            def _(stage=stage, j=j):
-                stage(j)
-
-        return carry
-
-    lax.fori_loop(0, chunks + max(lags), step, 0)
-
-    def settle(j, carry):
+    def settle(j):
         _, back, _ = sides(j)
         _, ring_from = ring_sides(j)
         sent = [far_copy(j), near_copy(j), sum_copy(j), ahead_copy(j, z), back_copy(j, z), on_copy(j, back),
@@ -320,10 +309,25 @@
         def _():
             mid_copy(lax.div(j, 2)).wait_send()
 
+    paired = (prepare, two_levels, last_level)
+    stages = (leaf, pass_on, first_state, prepare, ring_hand_on, two_levels, last_level, hand_on, finish, settle)
+
+    def step(s, carry):
+        for at in ORDER:
+            lag, stage = lags[at], stages[at]
+            j = s - lag
+            due = (j >= 0) & (j < chunks)
+            if stage in paired:
+                due = due & (lax.rem(j, 2) == 1)
+
+            @pl.when(due)
+            def _(stage=stage, j=j):
+                stage(j)
+
         return carry
 
+    lax.fori_loop(0, chunks + max(lags), step, 0)
     t_copy.wait_send()
-    lax.fori_loop(0, chunks, settle, 0)
 
 
 def mixed(rows, cid, plan, x, v, t, u):
@@ -334,7 +338,7 @@
     smem, vmem, hbm = (pl.BlockSpec(memory_space=m) for m in (pltpu.SMEM, pltpu.VMEM, pltpu.HBM))
     x = x.reshape(4, 2, batches // 8, orders, fields, points)
     arrays = [
-        *[((4, *x.shape[2:]), BF16)] * 2, (v.shape, BF16), (t.shape, BF16), (u.shape, BF16),
+        *[(x.shape[2:], BF16)] * 8, (v.shape, BF16), (t.shape, BF16), (u.shape, BF16),
         ((rows, QUAD * 128), BF16), ((groups, rows, 128), BF16), ((4, groups, 2, rows, rows), BF16),
         *[(chunk, BF16)] * 6, *[(chunk, F32)] * 2,
         ((chunks, 4, rows, 128), BF16), *[((groups, 2, rows, 128), BF16)] * 2, ((chunks, 4, rows, 128), BF16),
@@ -351,7 +355,7 @@
             pltpu.SemaphoreType.DMA((10, chunks)),
             pltpu.SemaphoreType.DMA,
             pltpu.SemaphoreType.DMA,
-            pltpu.SemaphoreType.DMA((5,)),
+            pltpu.SemaphoreType.DMA((11,)),
         ],
         compiler_params=pltpu.CompilerParams(
             collective_id=cid, has_side_effects=True, vmem_limit_bytes=size + 13 * 2**20),

time: 70 us -> 72.8 us (1.040)
  Pallas kernels: 68.7 us -> 71.4 us
    pallas_call x1, Pallas kernels: 63 us -> 65.7 us  [mixed(): pl.pallas_call(functools.partial(mixing, rows, LAGS), out_shape=jax.Shape...]
where the time goes in v4:
time: 72.8 us; the launch traced here: 72.6 us
  Pallas kernels  71.4 us (98%)
  between operations  0.85 us (1%)
    pallas_call x1, Pallas kernels, mixed(): pl.pallas_call(functools.partial(mixing, rows, LAGS), out_shape=jax.Shape...  65.7 us
    pallas_call x1, Pallas kernels, dealt_out(): pl.pallas_call(dealing, out_shape=jax.ShapeDtypeStruct(shape, BF16), in_s...  4.11 us
    pallas_call x1, Pallas kernels, planned(): pl.pallas_call(functools.partial(planning, heights), out_shape=(jax.Shape...  1.58 us

profile of v4, /device:TPU:0, one launch (start us, length us, event | category | flops | bytes accessed | tf_op | source)
XLA Modules:
  0.0 72.6 jit_solution(9842776641994914097)
XLA Ops:
  0.0 1.6 %shard_map.64 = (s32[4,32]{1,0:T(4,128)S(1)}, s32[1]{0:T(128)}) custom-call(s32[32]{0:T(128)} %orders.1, s32[32]{0:T(128)} %ranks.1), custom_call_target="tpu_custom_call" | custom-call | tf_op jit(solution)/shard_map/pallas_call | solution.py:436
  2.2 70.2 %conditional.1 = (bf16[16,32,64,128]{3,2,1,0:T(8,128)(2,1)}) conditional(s32[]{:T(128)} %bitcast.4, (bf16[16,32,64,128]{3,2,1,0:T(8,128)(2,1)}, s32[4,32]{1,0:T(4,128)S(1)}, bf16[32,64,128]{2,1,0:T(8,128)(2,1)}, bf16[3,32,1,64,128]{4,3,2,1,0:T(8,128)(2,1)}, bf16[32,64,128]{2,1,0:T(8,128)(2,1)}) %tuple.17, ...), branch_computations={%region_0.0_spmd, %region_1.0_spmd, %region_2.0_spmd, %region_3.0_... | conditional | flops 1000000000 | bytes 50331684 | solution.py:453
  2.3 65.7 %branch_2_fun.2.packed = bf16[8,4,16,64,128]{4,3,2,1,0:T(8,128)(2,1)S(1)} custom-call(s32[4,32]{1,0:T(4,128)S(1)} %get-tuple-element.60.plan, bf16[4,2,2,32,64,128]{5,4,3,2,1,0:T(8,128)(2,1)} %bitcast.7, bf16[32,64,128]{2,1,0:T(8,128)(2,1)} %get-tuple-element.62.v_hbm, bf16[3,32,1,64,128]{4,3,2,1,0:T(8,128)(2,1)} %get-tuple-element.63.t_hbm, ...), custom_call_target="tpu_custom_call" | custom-call | flops 1000000000 | bytes 16777216 | tf_op jit(solution)/shard_map/cond/branch_2_fun/pallas_call | solution.py:347
  67.9 4.1 %branch_2_fun.3 = bf16[16,32,64,128]{3,2,1,0:T(8,128)(2,1)} custom-call(s32[4,32]{1,0:T(4,128)S(1)} %get-tuple-element.60.plan, bf16[8,4,16,64,128]{4,3,2,1,0:T(8,128)(2,1)S(1)} %branch_2_fun.2.packed), custom_call_target="tpu_custom_call" | custom-call | tf_op jit(solution)/shard_map/cond/branch_2_fun/pallas_call | solution.py:378
  (1 shorter events, 0.0 us)

commit v5 on v4

--- a/solution.py
+++ b/solution.py
@@ -406,7 +406,6 @@
     n = ranks.shape[0]
     groups = n // QUAD
     i, j = (lax.broadcasted_iota(I32, (n, n), d).astype(F32) for d in (0, 1))
-    lane = lax.broadcasted_iota(I32, (1, n), 1).astype(F32)
     rank = ranks[...].reshape(1, n).astype(F32)
     order = orders[...].reshape(1, n).astype(F32)
     rank_down, order_down = turned(rank), turned(order)
@@ -422,9 +421,9 @@
         return jnp.sum(jnp.where(here, values, 0.0), axis=0, keepdims=True)
 
     rank_here = dealt(rank_down)
-    group = sum(jnp.where(lane >= QUAD * m, 1.0, 0.0) for m in range(1, groups))
-    earlier = (turned(group) == group) & (i < j)
-    first = jnp.sum(jnp.where(earlier, turned(rank_here), 0.0), axis=0, keepdims=True)
+    group, group_down = (sum(jnp.where(at >= QUAD * m, 1.0, 0.0) for m in range(1, groups)) for at in (j, i))
+    rank_here_down = jnp.sum(jnp.where(slot == i, rank, 0.0), axis=1, keepdims=True)
+    first = jnp.sum(jnp.where((group_down == group) & (i < j), rank_here_down, 0.0), axis=0, keepdims=True)
     for at, row in enumerate((dealt(i), first, rank_here, dealt(order_down))):
         plan[at:at + 1, :] = row.astype(I32)
     most = jnp.max(first + rank_here)

time: 72.8 us -> 68.4 us (0.940); the launches traced: 72.6 us -> 69 us
  Pallas kernels: 71.4 us -> 67.9 us
    pallas_call x1, Pallas kernels: 65.7 us -> 62.3 us  [mixed(): pl.pallas_call(functools.partial(mixing, rows, LAGS), out_shape=jax.Shape...]
where the time goes in v5:
time: 68.4 us; the launch traced here: 69 us
  Pallas kernels  67.9 us (99%)
  between operations  0.85 us (1%)
    pallas_call x1, Pallas kernels, mixed(): pl.pallas_call(functools.partial(mixing, rows, LAGS), out_shape=jax.Shape...  62.3 us
    pallas_call x1, Pallas kernels, dealt_out(): pl.pallas_call(dealing, out_shape=jax.ShapeDtypeStruct(shape, BF16), in_s...  4.11 us
    pallas_call x1, Pallas kernels, planned(): pl.pallas_call(functools.partial(planning, heights), out_shape=(jax.Shape...  1.49 us

profile of v5, /device:TPU:0, one launch (start us, length us, event | category | flops | bytes accessed | tf_op | source)
XLA Modules:
  0.0 69.0 jit_solution(5384655940276063221)
XLA Ops:
  0.0 1.5 %shard_map.64 = (s32[4,32]{1,0:T(4,128)S(1)}, s32[1]{0:T(128)}) custom-call(s32[32]{0:T(128)} %orders.1, s32[32]{0:T(128)} %ranks.1), custom_call_target="tpu_custom_call" | custom-call | tf_op jit(solution)/shard_map/pallas_call | solution.py:435
  2.2 66.7 %conditional.1 = (bf16[16,32,64,128]{3,2,1,0:T(8,128)(2,1)}) conditional(s32[]{:T(128)} %bitcast.4, (bf16[16,32,64,128]{3,2,1,0:T(8,128)(2,1)}, s32[4,32]{1,0:T(4,128)S(1)}, bf16[32,64,128]{2,1,0:T(8,128)(2,1)}, bf16[3,32,1,64,128]{4,3,2,1,0:T(8,128)(2,1)}, bf16[32,64,128]{2,1,0:T(8,128)(2,1)}) %tuple.17, ...), branch_computations={%region_0.0_spmd, %region_1.0_spmd, %region_2.0_spmd, %region_3.0_... | conditional | flops 1000000000 | bytes 50331684 | solution.py:452
  2.2 62.3 %branch_1_fun.2.packed = bf16[8,4,16,64,128]{4,3,2,1,0:T(8,128)(2,1)S(1)} custom-call(s32[4,32]{1,0:T(4,128)S(1)} %get-tuple-element.55.plan, bf16[4,2,2,32,64,128]{5,4,3,2,1,0:T(8,128)(2,1)} %bitcast.6, bf16[32,64,128]{2,1,0:T(8,128)(2,1)} %get-tuple-element.57.v_hbm, bf16[3,32,1,64,128]{4,3,2,1,0:T(8,128)(2,1)} %get-tuple-element.58.t_hbm, ...), custom_call_target="tpu_custom_call" | custom-call | flops 1000000000 | bytes 16777216 | tf_op jit(solution)/shard_map/cond/branch_1_fun/pallas_call | solution.py:347
  64.5 4.1 %branch_1_fun.3 = bf16[16,32,64,128]{3,2,1,0:T(8,128)(2,1)} custom-call(s32[4,32]{1,0:T(4,128)S(1)} %get-tuple-element.55.plan, bf16[8,4,16,64,128]{4,3,2,1,0:T(8,128)(2,1)S(1)} %branch_1_fun.2.packed), custom_call_target="tpu_custom_call" | custom-call | tf_op jit(solution)/shard_map/cond/branch_1_fun/pallas_call | solution.py:378
  (1 shorter events, 0.0 us)

commit v6 on v5

--- a/solution.py
+++ b/solution.py
@@ -426,7 +426,7 @@
     first = jnp.sum(jnp.where((group_down == group) & (i < j), rank_here_down, 0.0), axis=0, keepdims=True)
     for at, row in enumerate((dealt(i), first, rank_here, dealt(order_down))):
         plan[at:at + 1, :] = row.astype(I32)
-    most = jnp.max(first + rank_here)
+    most = jnp.max(jnp.sum(jnp.where(group_down == group, rank_here_down, 0.0), axis=0, keepdims=True))
     pick[0] = sum((most > height).astype(I32) for height in heights[:-1])
 
 

time: 68.4 us -> 68.4 us (level)
  no operation moved by 1% of the time
where the time goes in v6:
time: 68.4 us; the launch traced here: 69 us
  Pallas kernels  67.9 us (99%)
  between operations  0.85 us (1%)
    pallas_call x1, Pallas kernels, mixed(): pl.pallas_call(functools.partial(mixing, rows, LAGS), out_shape=jax.Shape...  62.3 us
    pallas_call x1, Pallas kernels, dealt_out(): pl.pallas_call(dealing, out_shape=jax.ShapeDtypeStruct(shape, BF16), in_s...  4.11 us
    pallas_call x1, Pallas kernels, planned(): pl.pallas_call(functools.partial(planning, heights), out_shape=(jax.Shape...  1.49 us

profile of v6, /device:TPU:0, one launch (start us, length us, event | category | flops | bytes accessed | tf_op | source)
XLA Modules:
  0.0 69.0 jit_solution(4816153575923922160)
XLA Ops:
  0.0 1.5 %shard_map.64 = (s32[4,32]{1,0:T(4,128)S(1)}, s32[1]{0:T(128)}) custom-call(s32[32]{0:T(128)} %orders.1, s32[32]{0:T(128)} %ranks.1), custom_call_target="tpu_custom_call" | custom-call | tf_op jit(solution)/shard_map/pallas_call | solution.py:435
  2.1 66.7 %conditional.1 = (bf16[16,32,64,128]{3,2,1,0:T(8,128)(2,1)}) conditional(s32[]{:T(128)} %bitcast.4, (bf16[16,32,64,128]{3,2,1,0:T(8,128)(2,1)}, s32[4,32]{1,0:T(4,128)S(1)}, bf16[32,64,128]{2,1,0:T(8,128)(2,1)}, bf16[3,32,1,64,128]{4,3,2,1,0:T(8,128)(2,1)}, bf16[32,64,128]{2,1,0:T(8,128)(2,1)}) %tuple.17, ...), branch_computations={%region_0.0_spmd, %region_1.0_spmd, %region_2.0_spmd, %region_3.0_... | conditional | flops 1000000000 | bytes 50331684 | solution.py:452
  2.2 62.3 %branch_1_fun.2.packed = bf16[8,4,16,64,128]{4,3,2,1,0:T(8,128)(2,1)S(1)} custom-call(s32[4,32]{1,0:T(4,128)S(1)} %get-tuple-element.55.plan, bf16[4,2,2,32,64,128]{5,4,3,2,1,0:T(8,128)(2,1)} %bitcast.6, bf16[32,64,128]{2,1,0:T(8,128)(2,1)} %get-tuple-element.57.v_hbm, bf16[3,32,1,64,128]{4,3,2,1,0:T(8,128)(2,1)} %get-tuple-element.58.t_hbm, ...), custom_call_target="tpu_custom_call" | custom-call | flops 1000000000 | bytes 16777216 | tf_op jit(solution)/shard_map/cond/branch_1_fun/pallas_call | solution.py:347
  64.5 4.1 %branch_1_fun.3 = bf16[16,32,64,128]{3,2,1,0:T(8,128)(2,1)} custom-call(s32[4,32]{1,0:T(4,128)S(1)} %get-tuple-element.55.plan, bf16[8,4,16,64,128]{4,3,2,1,0:T(8,128)(2,1)S(1)} %branch_1_fun.2.packed), custom_call_target="tpu_custom_call" | custom-call | tf_op jit(solution)/shard_map/cond/branch_1_fun/pallas_call | solution.py:378
  (1 shorter events, 0.0 us)
